TPU v7x, 256 devices: a whole 4x4x8 slice. The times are simulated.
256 devices in a mesh: rep: 32 (over x, z), tp: 8 (over y, core).
Axes of the slice: x: 4, y: 4, z: 8, core: 2. Of those that a mesh axis runs over, the one named last changes fastest.
Arguments:
- res_state: bfloat16 [128, 128, 64, 128], P('rep', 'tp'), may hold values from -0.59765625 to 0.59765625
- res_conv_x: bfloat16 [128, 3, 8192], P('rep', None, 'tp'), may hold values from -6 to 6
- res_conv_bc: bfloat16 [128, 3, 2, 1024], P('rep', None, None, 'tp'), may hold values from -6 to 6
- res_x: bfloat16 [128, 64, 8192], P('rep', None, 'tp'), may hold values from -6 to 6
- res_bc: bfloat16 [128, 64, 2, 1024], P('rep', None, None, 'tp'), may hold values from -6 to 6
- res_z: bfloat16 [128, 64, 8192], P('rep', None, 'tp'), may hold values from -6 to 6
- res_dt: bfloat16 [128, 64, 128], P('rep', None, 'tp'), may hold values from -3 to 3
- res_count: int32 [32], P('rep'), may hold values from 1 to 4, as said below
- hand_state: bfloat16 [32, 128, 64, 128], P('rep', 'tp'), may hold values from -0.59765625 to 0.59765625
- hand_conv_x: bfloat16 [32, 3, 8192], P('rep', None, 'tp'), may hold values from -6 to 6
- hand_conv_bc: bfloat16 [32, 3, 2, 1024], P('rep', None, None, 'tp'), may hold values from -6 to 6
- slot_x: bfloat16 [96, 64, 8192], P('rep', None, 'tp'), may hold values from -6 to 6
- slot_bc: bfloat16 [96, 64, 2, 1024], P('rep', None, None, 'tp'), may hold values from -6 to 6
- slot_z: bfloat16 [96, 64, 8192], P('rep', None, 'tp'), may hold values from -6 to 6
- slot_dt: bfloat16 [96, 64, 128], P('rep', None, 'tp'), may hold values from -3 to 3
- assignment: int32 [32], replicated, may hold values from 0 to 31, as said below
- conv_wx: float32 [4, 8192], P(None, 'tp'), may hold values from -3 to 3
- conv_wbc: float32 [4, 2, 1024], P(None, None, 'tp'), may hold values from -3 to 3
- dt_bias: float32 [128], P('tp'), may hold values from -3 to 0.5
- a_log: float32 [128], P('tp'), may hold values from -2 to 1.2
- d_skip: float32 [128], P('tp'), may hold values from 0.5 to 1.5
- norm_w: float32 [8192], P('tp'), may hold values from 0.5 to 1.5
- out_w: bfloat16 [8192, 4096], P('tp'), may hold values from -0.0625 to 0.0625
Outputs:
- res_out: bfloat16 [128, 64, 4096], P('rep', None, 'tp')
- slot_out: bfloat16 [96, 64, 4096], P('rep', None, 'tp')
- slot_state: bfloat16 [96, 128, 64, 128], P('rep', 'tp')
Inputs may be any that keep to these rules, and one draw needn't show every extreme that they name: `assignment`: request r's handed state starts on replica index r. Each replica receives at most 3 requests and some replica exactly 3. Slot j of a replica serves its j-th request in order of r; inputs of its unused slots are ignored. `res_count`: resident slots j >= the replica's count are spare and give zeros; some replica has exactly 4.
All inputs are finite; a program needn't handle non-finite values.
Results may differ from a plain program's by a relative error of at most 0.019.
Values may be sent and summed in bfloat16 or wider, within the bound.
No kernel may reach another device: no remote copies, remote signals or barrier semaphores. Data moves between devices by JAX's collectives and lax.ppermute only.
A program may use at most 128 MiB of HBM per device.

v0:
```python
import functools

import jax
import jax.numpy as jnp
from jax import lax
from jax.experimental import pallas as pl
from jax.experimental.pallas import tpu as pltpu
from jax.sharding import PartitionSpec as P

F32 = jnp.float32
BF16 = jnp.bfloat16
ROWS = 64
INNER = 1024
STATE = 128
HEADS = 16
PAIRS = HEADS // 2
TAPS = 4
CAP = 3
NX, NZ = 4, 8
NY = 4
TOP = 8
PACK = 1056
EARLY = (0, 1, 7, 2, 6)
LATE = (3, 5, 4)
ORDER = EARLY + LATE
FIRST = ((1, 0), (3, 0))
SECOND = ((1, 1), (3, 1), (2, 0), (2, 1))
SPARE = ((1, 2), (3, 2), (1, 3), (3, 3), (2, 2))
SENDS = FIRST + SECOND + SPARE
VMEM_LIMIT = 58 * 1024 * 1024


def lanes_of(shape):
    return lax.broadcasted_iota(jnp.int32, shape, 1)


def rows_of(shape):
    return lax.broadcasted_iota(jnp.int32, shape, 0)


def mix_rows(win_x, win_bc, dt_pad, gated, dt, z_ref, params, load_state, store_state, normed, slot):
    wx, wbc, dt_bias, a_log, d_skip, norm_w = params
    coeffs = []
    for part in range(2):
        cols = slice(part * STATE, part * STATE + STATE)
        acc = win_bc[TOP - 3 : TOP - 3 + ROWS, cols] * wbc[0, part : part + 1, :]
        for k in range(1, TAPS):
            acc += win_bc[TOP - 3 + k : TOP - 3 + k + ROWS, cols] * wbc[k, part : part + 1, :]
        coeffs.append((acc / (1.0 + jnp.exp(-acc))).astype(BF16))
    coeff_b, coeff_c = coeffs

    dt_pad[...] = jnp.zeros_like(dt_pad)
    dt_pad[0:HEADS, 0:ROWS] = dt[0].astype(F32)
    raw = dt_pad[...].T[0:ROWS, 0:HEADS] + dt_bias[...]
    step = jnp.maximum(raw, 0.0) + jnp.log(1.0 + jnp.exp(-jnp.abs(raw)))
    dt_pad[...] = jnp.zeros_like(dt_pad)
    dt_pad[0:ROWS, 0:HEADS] = step
    dt_pad[ROWS:, 0:HEADS] = step * -jnp.exp(a_log[...])
    size = dt_pad[0:ROWS]
    cum = dt_pad[ROWS:]
    row = rows_of((ROWS, 128))
    for shift in (1, 2, 4, 8, 16, 32):
        cum = cum + jnp.where(row >= shift, pltpu.roll(cum, shift, 0), 0.0)

    lane = lanes_of((ROWS, 128))
    left = lane < 64
    source = jnp.where(left, lane, lane - 64)
    causal = row >= source
    diagonal = row == source
    twice_b = jnp.concatenate([coeff_b, coeff_b], axis=0)
    scores = lax.dot_general(
        coeff_c, twice_b, (((1,), (1,)), ((), ())), preferred_element_type=F32
    )
    squares = jnp.zeros((ROWS, 128), F32)
    for pair in range(PAIRS):
        cols = slice(pair * 128, pair * 128 + 128)
        first, second = 2 * pair, 2 * pair + 1

        def spread(values):
            return jnp.where(left, values[:, first : first + 1], values[:, second : second + 1])

        acc = win_x[TOP - 3 : TOP - 3 + ROWS, cols] * wx[0:1, cols]
        for k in range(1, TAPS):
            acc += win_x[TOP - 3 + k : TOP - 3 + k + ROWS, cols] * wx[k : k + 1, cols]
        x_conv = acc / (1.0 + jnp.exp(-acc))
        cum_here = spread(cum)
        x_size = x_conv * spread(size)
        cum_source = jnp.sum(jnp.where(diagonal, cum_here, 0.0), axis=0, keepdims=True)
        decay = jnp.where(causal, jnp.exp(jnp.where(causal, cum_here - cum_source, 0.0)), 0.0)
        weights = (decay * scores).astype(BF16)
        blocks = jnp.concatenate(
            [jnp.where(left, x_size, 0.0), jnp.where(left, 0.0, x_size)], axis=0
        ).astype(BF16)
        y = jnp.dot(weights, blocks, preferred_element_type=F32)
        held = load_state(pair)
        y += jnp.exp(cum_here) * lax.dot_general(
            coeff_c, held, (((1,), (1,)), ((), ())), preferred_element_type=F32
        )
        y += spread(d_skip[...]) * x_conv
        if store_state is not None:
            last = cum_here[ROWS - 1 : ROWS, :]
            tail = (jnp.exp(last - cum_here) * x_size).astype(BF16)
            update = lax.dot_general(
                tail, coeff_b, (((0,), (0,)), ((), ())), preferred_element_type=F32
            )
            final = jnp.exp(cum[ROWS - 1 : ROWS, :])
            keep = jnp.where(
                rows_of((128, 128)) < 64, final[:, first : first + 1], final[:, second : second + 1]
            )
            store_state(pair, held.astype(F32) * keep + update)
        gate = z_ref[0, :, cols].astype(F32)
        g = y * (gate / (1.0 + jnp.exp(-gate)))
        gated[:, cols] = g
        squares += g * g
    scale = lax.rsqrt(jnp.sum(squares, axis=1, keepdims=True) * (1.0 / INNER) + 1e-05)
    normed[pl.ds(slot * ROWS, ROWS), :] = (gated[...] * scale * norm_w[...]).astype(BF16)


def load_pairs(win_bc, bc):
    both = bc[0].astype(F32)
    win_bc[TOP:, :STATE] = both[:, 0, :]
    win_bc[TOP:, STATE:] = both[:, 1, :]


def project(blocks, normed, weight, sent, kept):
    width = sent.shape[2]
    for at, out in ((0, sent), (NY, kept)):
        for k in range(NY):
            start = pl.multiple_of(blocks[at + k] * width, width)
            out[k] = jnp.dot(
                normed[...], weight[:, pl.ds(start, width)], preferred_element_type=F32
            ).astype(BF16)


def resident_kernel(
    count, blocks, out_w, state, conv_x, conv_bc, x, bc, z, dt,
    wx, wbc, dt_bias, a_log, d_skip, norm_w, parts, conv_rows, normed, weight,
    weight_sem, win_x, win_bc, dt_pad, gated,
):
    slot = pl.program_id(0)
    fetch = pltpu.make_async_copy(out_w, weight, weight_sem)

    @pl.when(slot == 0)
    def _():
        fetch.start()
        conv_rows[...] = conv_x[...].astype(F32)

    @pl.when(slot < count[0])
    def _():
        for k in range(TAPS - 1):
            win_x[TOP - 3 + k : TOP - 2 + k, :] = conv_rows[k, pl.ds(slot, 1), :]
        win_x[TOP:, :] = x[0].astype(F32)
        for k in range(TAPS - 1):
            both = conv_bc[0, k].astype(F32)
            for part in range(2):
                win_bc[TOP - 3 + k : TOP - 2 + k, part * STATE : part * STATE + STATE] = both[
                    part : part + 1
                ]
        load_pairs(win_bc, bc)

        def load_state(pair):
            return state[0, 2 * pair : 2 * pair + 2].reshape(128, STATE)

        mix_rows(
            win_x, win_bc, dt_pad, gated, dt, z,
            (wx, wbc, dt_bias, a_log, d_skip, norm_w), load_state, None, normed, slot,
        )

    @pl.when(slot >= count[0])
    def _():
        normed[pl.ds(slot * ROWS, ROWS), :] = jnp.zeros((ROWS, INNER), BF16)

    @pl.when(slot == pl.num_programs(0) - 1)
    def _():
        fetch.wait()
        project(blocks, normed, weight, parts.at[0:NY], parts.at[NY:])


ROW_SCRATCH = [
    pltpu.VMEM((TOP + ROWS, INNER), F32),
    pltpu.VMEM((TOP + ROWS, 2 * STATE), F32),
    pltpu.VMEM((2 * ROWS, 128), F32),
    pltpu.VMEM((ROWS, INNER), F32),
]


def whole(array):
    return pl.BlockSpec(array.shape, lambda *_: (0,) * array.ndim)


def per_slot(shape):
    return pl.BlockSpec((1,) + shape, lambda i, *_: (i,) + (0,) * len(shape))


def row_scratch(slots):
    return [
        pltpu.VMEM((slots * ROWS, INNER), BF16),
        pltpu.VMEM((INNER, 4096), BF16),
        pltpu.SemaphoreType.DMA,
    ] + ROW_SCRATCH


def partial_sums(slots):
    shape = (NY, slots * ROWS, 4096 // 8)
    return [jax.ShapeDtypeStruct(shape, BF16)] * 2


def resident_rows(count, blocks, out_w, state, conv_x, conv_bc, x, bc, z, dt, params):
    slots = state.shape[0]
    parts = jax.ShapeDtypeStruct((2 * NY, slots * ROWS, out_w.shape[1] // 8), BF16)
    return pl.pallas_call(
        resident_kernel,
        grid=(slots,),
        in_specs=[pl.BlockSpec(memory_space=pltpu.SMEM)] * 2
        + [pl.BlockSpec(memory_space=pl.ANY), per_slot(state.shape[1:]), whole(conv_x)]
        + [per_slot(a.shape[1:]) for a in (conv_bc, x, bc, z, dt)]
        + [whole(a) for a in params],
        out_specs=whole(parts),
        out_shape=parts,
        scratch_shapes=[pltpu.VMEM((TAPS - 1, slots, INNER), F32)] + row_scratch(slots),
        compiler_params=pltpu.CompilerParams(vmem_limit_bytes=VMEM_LIMIT),
        cost_estimate=pl.CostEstimate(
            flops=3_000_000_000, bytes_accessed=16_000_000, transcendentals=0
        ),
        name="resident_rows",
    )(count, blocks, out_w, state, conv_x, conv_bc, x, bc, z, dt, *params)


def line_hits(assign, target, column):
    target_z = lax.rem(target, NZ)
    return [
        (assign[column * NZ + lax.rem(target_z + NZ - offset, NZ)] == target).astype(jnp.int32)
        for offset in ORDER
    ]


def send_ranks(hits, shift):
    seen = jnp.int32(0)
    if shift != 2:
        seen = 1 - functools.reduce(jnp.maximum, hits[: len(EARLY)])
    ranks = []
    for hit in hits:
        ranks.append(seen)
        seen = seen + hit
    return ranks


def forward_kernel(sends, offsets, info, *refs):
    packets = dict(zip(offsets, refs))
    outs, sems = refs[len(offsets) : -1], refs[-1]
    me = info[32]
    column, z = lax.div(me, NZ), lax.rem(me, NZ)
    todo = []
    for slot, (shift, wanted) in enumerate(sends):
        target = lax.rem(column + shift, NX) * NZ + z
        hits = line_hits(info, target, column)
        for offset, hit, rank in zip(ORDER, hits, send_ranks(hits, shift)):
            if offset in packets:
                todo.append(
                    ((hit == 1) & (rank == wanted),
                     pltpu.make_async_copy(packets[offset], outs[slot], sems.at[slot]))
                )
    if 4 not in offsets:
        slot = len(sends)
        even = lax.rem(z, 2) == 0
        for when, offset in ((even, 2), (jnp.logical_not(even), 6)):
            todo.append(
                (when, pltpu.make_async_copy(packets[offset], outs[slot], sems.at[slot]))
            )
    for wanted, copy in todo:
        pl.when(wanted)(copy.start)
    for wanted, copy in todo:
        pl.when(wanted)(copy.wait)


def forward(sends, offsets, info, packets):
    count = len(sends) + (0 if 4 in offsets else 1)
    return pl.pallas_call(
        functools.partial(forward_kernel, sends, offsets),
        in_specs=[pl.BlockSpec(memory_space=pltpu.SMEM)]
        + [pl.BlockSpec(memory_space=pl.ANY)] * len(packets),
        out_specs=[pl.BlockSpec(memory_space=pl.ANY)] * count,
        out_shape=[jax.ShapeDtypeStruct((PACK, 128), BF16)] * count,
        scratch_shapes=[pltpu.SemaphoreType.DMA((count,))],
        cost_estimate=pl.CostEstimate(flops=0, bytes_accessed=3_000_000, transcendentals=0),
        name="forward",
    )(info, *packets)


def blank_kernel(info, *outs):
    pass


def blank(info, count):
    return pl.pallas_call(
        blank_kernel,
        in_specs=[pl.BlockSpec(memory_space=pltpu.SMEM)],
        out_specs=[pl.BlockSpec(memory_space=pl.ANY)] * count,
        out_shape=[jax.ShapeDtypeStruct((PACK, 128), BF16)] * count,
        name="blank",
    )(info)


PACKETS = len(ORDER)
ARRIVED = len(SENDS)


def slot_kernel(info, blocks, out_w, *refs):
    line, rest = refs[:PACKETS], refs[PACKETS:]
    came, rest = rest[:ARRIVED], rest[ARRIVED:]
    (x, bc, z, dt, wx, wbc, dt_bias, a_log, d_skip, norm_w, sent, kept, state,
     held, valid, sems, normed, weight, weight_sem, win_x, win_bc, dt_pad, gated) = rest
    fetch = pltpu.make_async_copy(out_w, weight, weight_sem)
    packets = dict(zip(ORDER, line))
    arrived = dict(zip(SENDS, came))
    slot = pl.program_id(0)
    me = info[32]
    column, my_z = lax.div(me, NZ), lax.rem(me, NZ)

    @pl.when(slot == 0)
    def _():
        before = jnp.int32(0)
        for request in range(NX * NZ):
            valid[request] = before
            before = before + (info[request] == me).astype(jnp.int32)
        valid[NX * NZ] = before
        for shift in range(NX):
            sender = lax.rem(column + NX - shift, NX)
            hits = line_hits(info, me, sender)
            for offset, hit, rank in zip(ORDER, hits, send_ranks(hits, shift)):
                source = sender * NZ + lax.rem(my_z + NZ - offset, NZ)
                place = valid[source]

                @pl.when(hit == 1)
                def _(shift=shift, offset=offset, rank=rank, place=place):
                    if shift == 0:
                        pltpu.make_async_copy(
                            packets[offset], held.at[place], sems.at[place]
                        ).start()
                    for (over, n), packet in arrived.items():
                        if over == shift:
                            @pl.when(rank == n)
                            def _(packet=packet):
                                pltpu.make_async_copy(
                                    packet, held.at[place], sems.at[place]
                                ).start()
        fetch.start()

    live = slot < valid[NX * NZ]

    @pl.when(live)
    def _():
        win_x[TOP:, :] = x[0].astype(F32)
        load_pairs(win_bc, bc)
        pltpu.make_async_copy(held.at[slot], held.at[slot], sems.at[slot]).wait()
        conv = held[slot, 1024:PACK, :].astype(F32)
        for k in range(TAPS - 1):
            for b in range(8):
                win_x[TOP - 3 + k : TOP - 2 + k, 128 * b : 128 * b + 128] = conv[
                    8 * k + b : 8 * k + b + 1
                ]
            for b in range(2):
                win_bc[TOP - 3 + k : TOP - 2 + k, 128 * b : 128 * b + 128] = conv[
                    24 + 2 * k + b : 25 + 2 * k + b
                ]

        def load_state(pair):
            return held[slot, 128 * pair : 128 * pair + 128, :]

        def store_state(pair, value):
            state[0, 2 * pair : 2 * pair + 2] = value.astype(BF16).reshape(2, 64, STATE)

        mix_rows(
            win_x, win_bc, dt_pad, gated, dt, z,
            (wx, wbc, dt_bias, a_log, d_skip, norm_w), load_state, store_state, normed, slot,
        )

    @pl.when(jnp.logical_not(live))
    def _():
        normed[pl.ds(slot * ROWS, ROWS), :] = jnp.zeros((ROWS, INNER), BF16)
        state[...] = jnp.zeros_like(state)

    @pl.when(slot == pl.num_programs(0) - 1)
    def _():
        fetch.wait()
        project(blocks, normed, weight, sent, kept)


def slot_rows(info, blocks, out_w, line, came, x, bc, z, dt, params):
    slots = x.shape[0]
    sums = partial_sums(slots)
    return pl.pallas_call(
        slot_kernel,
        grid=(slots,),
        in_specs=[pl.BlockSpec(memory_space=pltpu.SMEM)] * 2
        + [pl.BlockSpec(memory_space=pl.ANY)] * (1 + PACKETS + ARRIVED)
        + [per_slot(a.shape[1:]) for a in (x, bc, z, dt)]
        + [whole(a) for a in params],
        out_specs=[whole(a) for a in sums] + [per_slot((HEADS, 64, STATE))],
        out_shape=sums + [jax.ShapeDtypeStruct((slots, HEADS, 64, STATE), BF16)],
        scratch_shapes=[
            pltpu.VMEM((CAP, PACK, 128), BF16),
            pltpu.SMEM((NX * NZ + 1,), jnp.int32),
            pltpu.SemaphoreType.DMA((CAP,)),
        ]
        + row_scratch(slots),
        compiler_params=pltpu.CompilerParams(vmem_limit_bytes=VMEM_LIMIT),
        cost_estimate=pl.CostEstimate(
            flops=3_000_000_000, bytes_accessed=20_000_000, transcendentals=0
        ),
        name="slot_rows",
    )(info, blocks, out_w, *line, *came, x, bc, z, dt, *params)


def across_cores(array):
    return lax.ppermute(array, "tp", [(t, t ^ 1) for t in range(2 * NY)])


def chip_sums(own, from_mate):
    return [own[k].astype(F32) + from_mate[k].astype(F32) for k in range(NY)]


def reduce_out(chip, slots):
    total = chip[0]
    for k in range(1, NY):
        shifted = [(t, (t + 2 * k) % (2 * NY)) for t in range(2 * NY)]
        total = total + lax.ppermute(chip[k].astype(BF16), "tp", shifted).astype(F32)
    return total.astype(BF16).reshape(slots, ROWS, -1)


def along_z(array, step):
    pairs = [(x * NZ + z, x * NZ + (z + step) % NZ) for x in range(NX) for z in range(NZ)]
    return lax.ppermute(array, "rep", pairs)


def across_z(array):
    pairs = [
        (x * NZ + z, x * NZ + (z + (2 if z % 2 == 0 else -2)) % NZ)
        for x in range(NX) for z in range(NZ)
    ]
    return lax.ppermute(array, "rep", pairs)


def along_x(sends, arrays):
    return [
        lax.ppermute(
            array, "rep",
            [(x * NZ + z, (x + shift) % NX * NZ + z) for x in range(NX) for z in range(NZ)],
        )
        for (shift, _), array in zip(sends, arrays)
    ]


def on_device(
    res_state, res_conv_x, res_conv_bc, res_x, res_bc, res_z, res_dt, res_count,
    hand_state, hand_conv_x, hand_conv_bc, slot_x, slot_bc, slot_z, slot_dt,
    assignment, conv_wx, conv_wbc, dt_bias, a_log, d_skip, norm_w, out_w,
):
    me = lax.axis_index("rep")
    tp = lax.axis_index("tp")
    info = jnp.concatenate([assignment, me[None].astype(jnp.int32)])
    packet = jnp.concatenate(
        [
            hand_state.reshape(-1, STATE),
            hand_conv_x.reshape(-1, STATE),
            hand_conv_bc.reshape(-1, STATE),
            jnp.zeros((2, STATE), BF16),
        ],
        axis=0,
    )
    up1, down1 = along_z(packet, 1), along_z(packet, -1)
    up2, down2 = along_z(packet, 2), along_z(packet, -2)

    params = (
        conv_wx, conv_wbc, dt_bias[None], a_log[None], d_skip[None],
        norm_w[None],
    )
    chip, core = tp // 2, tp % 2
    turns = (chip + jnp.arange(NY, dtype=jnp.int32)) % NY
    blocks = jnp.concatenate([2 * turns + 1 - core, 2 * turns + core])
    res_blocks = jnp.arange(2 * NY, dtype=jnp.int32)
    res_parts = resident_rows(
        res_count, res_blocks, out_w, res_state, res_conv_x.transpose(1, 0, 2),
        res_conv_bc, res_x, res_bc, res_z, res_dt.transpose(0, 2, 1), params,
    )
    up1, down1, up2, down2, res_parts = lax.optimization_barrier(
        (up1, down1, up2, down2, res_parts)
    )
    early = [packet, up1, down1, up2, down2]
    *ahead, far = forward(FIRST, EARLY, info, early)
    far = across_z(far)
    up3, down3 = along_z(up2, 1), along_z(down2, -1)
    first = along_x(FIRST, ahead)
    up3, down3, far, *first = lax.optimization_barrier((up3, down3, far, *first))
    line = early + [up3, down3, far]
    ahead = forward(SECOND, ORDER, info, line)
    *ahead, info, res_parts = lax.optimization_barrier((*ahead, info, res_parts))
    res_parts = lax.all_to_all(res_parts, "tp", 0, 0, tiled=True)
    second = along_x(SECOND, ahead)

    ids = jnp.arange(NX * NZ)
    goes = assignment[None, :] == ids[:, None]
    offset = (ids[:, None] - ids[None, :]) % NZ
    far = (offset > 2) & (offset < 6)
    all_hits = jnp.sum(goes.reshape(-1, NX, NZ), axis=2)
    near_hits = jnp.sum((goes & ~far).reshape(-1, NX, NZ), axis=2)
    shift = (ids[:, None] // NZ - jnp.arange(NX)[None, :]) % NX
    room = jnp.where(shift == 2, 2, jnp.where(shift == 0, NZ, 1 + jnp.minimum(near_hits, 1)))
    more = jnp.any(all_hits > room)
    third = lax.cond(
        more,
        lambda *held: tuple(along_x(SPARE, forward(SPARE, ORDER, held[0], held[1:]))),
        lambda *held: tuple(blank(held[0], len(SPARE))),
        info, *line,
    )
    res_out = jnp.sum(res_parts.astype(F32), axis=0).astype(BF16)
    res_out = res_out.reshape(res_state.shape[0], ROWS, -1)
    sent, kept, slot_state = slot_rows(
        info, blocks, out_w, line, first + second + list(third), slot_x, slot_bc, slot_z,
        slot_dt.transpose(0, 2, 1), params,
    )
    slot_out = reduce_out(chip_sums(kept, across_cores(sent)), slot_x.shape[0])
    return res_out, slot_out, slot_state


def solution(mesh):
    rows = P("rep", None, "tp")
    pairs = P("rep", None, None, "tp")
    states = P("rep", "tp", None, None)
    return jax.shard_map(
        on_device,
        mesh=mesh,
        in_specs=(
            states, rows, pairs, rows, pairs, rows, rows, P("rep"),
            states, rows, pairs, rows, pairs, rows, rows,
            P(), P(None, "tp"), P(None, None, "tp"), P("tp"), P("tp"), P("tp"), P("tp"),
            P("tp", None),
        ),
        out_specs=(rows, rows, states),
        check_vma=False,
    )
```

profile of v0, /device:TPU:33, one launch (start us, length us, event | category | flops | bytes accessed | tf_op | source)
XLA Modules:
  0.0 104.4 jit_solution(7153456184948936646)
XLA Ops:
  0.6 0.7 reshape.104
  1.3 0.7 reshape.105
  2.0 1.0 concatenate.10.refs_0_
  3.1 1.7 %collective-permute-start.5 = (bf16[1056,128]{1,0:T(8,128)(2,1)S(1)}, bf16[1056,128]{1,0:T(8,128)(2,1)S(1)}, u32[]{:S(2)}, u32[]{:S(2)}) collective-permute-start(bf16[1056,128]{1,0:T(8,128)(2,1)S(1)} %concatenate.10.refs_0_), channel_id=1, source_target_pairs={{0,8},{8,16},{16,24},{24,32},{32,40},{40,48},{48,56},{56,0},{64,72... | collective-permute-start | bytes 811016 | tf_op jit(solution)/shard_map/ppermute | solution.py:433
  4.8 4.2 %collective-permute-start.7 = (bf16[1056,128]{1,0:T(8,128)(2,1)S(1)}, bf16[1056,128]{1,0:T(8,128)(2,1)S(1)}, u32[]{:S(2)}, u32[]{:S(2)}) collective-permute-start(bf16[1056,128]{1,0:T(8,128)(2,1)S(1)} %concatenate.10.refs_0_), channel_id=1, source_target_pairs={{0,16},{8,24},{16,32},{24,40},{32,48},{40,56},{48,0},{56,8},{64,80... | collective-permute-start | bytes 811016 | tf_op jit(solution)/shard_map/ppermute | solution.py:433
  9.0 0.7 collective-permute-start.8
  10.4 0.7 pad_add_fusion.info
  11.1 0.5 iota.40.blocks
  11.6 8.7 %resident_rows.1 = bf16[8,256,512]{2,1,0:T(8,128)(2,1)} custom-call(s32[1]{0:T(128)S(6)} %copy.36.count, s32[8]{0:T(128)} %iota.40.blocks, bf16[1024,4096]{1,0:T(8,128)(2,1)} %out_w.3, bf16[4,16,64,128]{3,2,1,0:T(8,128)(2,1)} %state.1, bf16[3,4,1024]{2,1,0:T(4,128)(2,1)} %bitcast.28, bf16[4,3,2,128]{3,2,1,0:T(2,128)(2,1)} %conv_bc.1, ...), custom_call_target="tpu_custom_call" | custom-call | flops 3000000000 | bytes 16000000 | tf_op jit(solution)/shard_map/resident_rows/pallas_call | solution.py:211
  20.4 0.0 collective-permute-done.5.refs_1_
  20.4 5.7 %collective-permute-done.7.refs_3_ = bf16[1056,128]{1,0:T(8,128)(2,1)S(1)} collective-permute-done((bf16[1056,128]{1,0:T(8,128)(2,1)S(1)}, bf16[1056,128]{1,0:T(8,128)(2,1)S(1)}, u32[]{:S(2)}, u32[]{:S(2)}) %collective-permute-start.7) | collective-permute-done | bytes 270368 | tf_op jit(solution)/shard_map/ppermute | solution.py:433
  26.1 0.0 collective-permute-done.8.refs_4_
  26.1 2.8 %collective-permute-start.9 = (bf16[1056,128]{1,0:T(8,128)(2,1)S(1)}, bf16[1056,128]{1,0:T(8,128)(2,1)}, u32[]{:S(2)}, u32[]{:S(2)}) collective-permute-start(bf16[1056,128]{1,0:T(8,128)(2,1)S(1)} %collective-permute-done.7.refs_3_), channel_id=1, source_target_pairs={{0,8},{8,16},{16,24},{24,32},{32,40},{40,48},{48,56},{56,0},{64,72... | collective-permute-start | bytes 811016 | tf_op jit(solution)/shard_map/ppermute | solution.py:433
  28.8 1.3 %forward.4 = (bf16[1056,128]{1,0:T(8,128)(2,1)}, bf16[1056,128]{1,0:T(8,128)(2,1)}, bf16[1056,128]{1,0:T(8,128)(2,1)}) custom-call(s32[33]{0:T(128)S(1)} %pad_add_fusion.info, bf16[1056,128]{1,0:T(8,128)(2,1)S(1)} %concatenate.10.refs_0_, bf16[1056,128]{1,0:T(8,128)(2,1)S(1)} %collective-permute-done.5.refs_1_, ...), custom_call_target="tpu_custom_call" | custom-call | bytes 3000000 | tf_op jit(solution)/shard_map/forward/pallas_call | solution.py:278
  30.2 0.9 collective-permute-start.11
  31.1 1.2 %collective-permute-start.12 = (bf16[1056,128]{1,0:T(8,128)(2,1)}, bf16[1056,128]{1,0:T(8,128)(2,1)S(1)}, u32[]{:S(2)}, u32[]{:S(2)}) collective-permute-start(bf16[1056,128]{1,0:T(8,128)(2,1)} %get-tuple-element.72), channel_id=1, source_target_pairs={{0,64},{8,72},{16,80},{24,88},{32,96},{40,104},{48,112},{56,120},{... | collective-permute-start | bytes 811016 | tf_op jit(solution)/shard_map/ppermute | solution.py:446
  32.3 1.5 %collective-permute-start.13 = (bf16[1056,128]{1,0:T(8,128)(2,1)}, bf16[1056,128]{1,0:T(8,128)(2,1)S(1)}, u32[]{:S(2)}, u32[]{:S(2)}) collective-permute-start(bf16[1056,128]{1,0:T(8,128)(2,1)} %get-tuple-element.73), channel_id=1, source_target_pairs={{0,192},{8,200},{16,208},{24,216},{32,224},{40,232},{48,240},{56,2... | collective-permute-start | bytes 811016 | tf_op jit(solution)/shard_map/ppermute | solution.py:446
  33.8 0.1 eq.37
  33.9 0.1 convert_reduce_fusion
  34.0 0.6 fusion.12
  35.3 0.0 collective-permute-done.9.refs_5_
  35.3 5.3 %collective-permute-done.11.refs_7_ = bf16[1056,128]{1,0:T(8,128)(2,1)} collective-permute-done((bf16[1056,128]{1,0:T(8,128)(2,1)}, bf16[1056,128]{1,0:T(8,128)(2,1)}, u32[]{:S(2)}, u32[]{:S(2)}) %collective-permute-start.11) | collective-permute-done | bytes 270368 | tf_op jit(solution)/shard_map/ppermute | solution.py:441
  40.6 0.0 collective-permute-done.12.refs_8_
  40.6 1.4 %forward.5 = (bf16[1056,128]{1,0:T(8,128)(2,1)}, bf16[1056,128]{1,0:T(8,128)(2,1)}, bf16[1056,128]{1,0:T(8,128)(2,1)}, bf16[1056,128]{1,0:T(8,128)(2,1)}) custom-call(s32[33]{0:T(128)S(1)} %pad_add_fusion.info, bf16[1056,128]{1,0:T(8,128)(2,1)S(1)} %concatenate.10.refs_0_, bf16[1056,128]{1,0:T(8,128)(2,1)S(1)} %collective-permute-done.5.refs_1_, ...), custom_call_target="tpu_custom_call" | custom-call | bytes 3000000 | tf_op jit(solution)/shard_map/forward/pallas_call | solution.py:278
  42.1 0.7 conditional.1
  42.1 0.5 blank.1
  42.8 0.7 collective-permute-start.14
  43.5 10.5 %collective-permute-start.15 = (bf16[1056,128]{1,0:T(8,128)(2,1)}, bf16[1056,128]{1,0:T(8,128)(2,1)}, u32[]{:S(2)}, u32[]{:S(2)}) collective-permute-start(bf16[1056,128]{1,0:T(8,128)(2,1)} %get-tuple-element.87), channel_id=1, source_target_pairs={{0,192},{8,200},{16,208},{24,216},{32,224},{40,232},{48,240},{56,2... | collective-permute-start | bytes 811016 | tf_op jit(solution)/shard_map/ppermute | solution.py:446
  54.1 1.1 %collective-permute-start.16 = (bf16[1056,128]{1,0:T(8,128)(2,1)}, bf16[1056,128]{1,0:T(8,128)(2,1)}, u32[]{:S(2)}, u32[]{:S(2)}) collective-permute-start(bf16[1056,128]{1,0:T(8,128)(2,1)} %get-tuple-element.88), channel_id=1, source_target_pairs={{0,128},{8,136},{16,144},{24,152},{32,160},{40,168},{48,176},{56,1... | collective-permute-start | bytes 811016 | tf_op jit(solution)/shard_map/ppermute | solution.py:446
  55.2 1.9 %collective-permute-start.17 = (bf16[1056,128]{1,0:T(8,128)(2,1)}, bf16[1056,128]{1,0:T(8,128)(2,1)}, u32[]{:S(2)}, u32[]{:S(2)}) collective-permute-start(bf16[1056,128]{1,0:T(8,128)(2,1)} %get-tuple-element.89), channel_id=1, source_target_pairs={{0,128},{8,136},{16,144},{24,152},{32,160},{40,168},{48,176},{56,1... | collective-permute-start | bytes 811016 | tf_op jit(solution)/shard_map/ppermute | solution.py:446
  57.1 8.3 %all-to-all-start = ((bf16[8,256,512]{2,1,0:T(8,128)(2,1)}), bf16[8,256,512]{2,1,0:T(8,128)(2,1)S(1)}, u32[]{:S(2)}, u32[]{:S(2)}) async-start(bf16[8,256,512]{2,1,0:T(8,128)(2,1)} %resident_rows.1), calls=%async_computation | async-start | bytes 4194304 | tf_op jit(solution)/shard_map/all_to_all | solution.py:498
  65.4 0.6 pad_add_fusion.1.blocks
  66.0 0.0 collective-permute-done.14.refs_10_
  66.0 4.4 %collective-permute-done.15.refs_11_ = bf16[1056,128]{1,0:T(8,128)(2,1)} collective-permute-done((bf16[1056,128]{1,0:T(8,128)(2,1)}, bf16[1056,128]{1,0:T(8,128)(2,1)}, u32[]{:S(2)}, u32[]{:S(2)}) %collective-permute-start.15) | collective-permute-done | bytes 270368 | tf_op jit(solution)/shard_map/ppermute | solution.py:446
  70.4 0.1 collective-permute-done.17.refs_13_
  70.5 8.2 %slot_rows.1 = (bf16[4,192,512]{2,1,0:T(8,128)(2,1)}, bf16[4,192,512]{2,1,0:T(8,128)(2,1)}, bf16[3,16,64,128]{3,2,1,0:T(8,128)(2,1)}) custom-call(s32[33]{0:T(128)S(1)} %pad_add_fusion.info, s32[8]{0:T(128)} %pad_add_fusion.1.blocks, bf16[1024,4096]{1,0:T(8,128)(2,1)} %out_w.3, bf16[1056,128]{1,0:T(8,128)(2,1)S(1)} %concatenate.10.refs_0_, ...), custom_call_target="tpu_custom_call" | custom-call | flops 3000000000 | bytes 20000000 | tf_op jit(solution)/shard_map/slot_rows/pallas_call | solution.py:392
  78.8 4.0 %collective-permute-start.18 = (bf16[4,192,512]{2,1,0:T(8,128)(2,1)}, bf16[4,192,512]{2,1,0:T(8,128)(2,1)S(1)}, u32[]{:S(2)}, u32[]{:S(2)}) collective-permute-start(bf16[4,192,512]{2,1,0:T(8,128)(2,1)} %get-tuple-element.96), channel_id=1, source_target_pairs={{0,1},{1,0},{2,3},{3,2},{4,5},{5,4},{6,7},{7,6},{8,9},{9,8},{10,11... | collective-permute-start | bytes 2359304 | tf_op jit(solution)/shard_map/ppermute | solution.py:416
  82.8 2.1 %collective-permute-done.18 = bf16[4,192,512]{2,1,0:T(8,128)(2,1)S(1)} collective-permute-done((bf16[4,192,512]{2,1,0:T(8,128)(2,1)}, bf16[4,192,512]{2,1,0:T(8,128)(2,1)S(1)}, u32[]{:S(2)}, u32[]{:S(2)}) %collective-permute-start.18) | collective-permute-done | bytes 786464 | tf_op jit(solution)/shard_map/ppermute | solution.py:416
  85.0 1.3 %fusion.3 = (bf16[192,512]{1,0:T(8,128)(2,1)S(1)}, bf16[192,512]{1,0:T(8,128)(2,1)S(1)}, bf16[192,512]{1,0:T(8,128)(2,1)S(1)}) fusion(bf16[4,192,512]{2,1,0:T(8,128)(2,1)S(1)} %collective-permute-done.18, bf16[4,192,512]{2,1,0:T(8,128)(2,1)} %get-tuple-element.95), kind=kLoop, calls=%fused_computation.7 | loop fusion | flops 1179648 | bytes 1769472 | tf_op jit(solution)/shard_map/convert_element_type | solution.py:427
  86.2 2.8 %collective-permute-start.21 = (bf16[192,512]{1,0:T(8,128)(2,1)S(1)}, bf16[192,512]{1,0:T(8,128)(2,1)S(1)}, u32[]{:S(2)}, u32[]{:S(2)}) collective-permute-start(bf16[192,512]{1,0:T(8,128)(2,1)S(1)} %get-tuple-element.101), channel_id=1, source_target_pairs={{0,6},{1,7},{2,0},{3,1},{4,2},{5,3},{6,4},{7,5},{8,14},{9,15},{10,... | collective-permute-start | bytes 589832 | tf_op jit(solution)/shard_map/ppermute | solution.py:427
  89.0 0.4 collective-permute-start.20
  89.4 0.7 collective-permute-start.19
  90.1 4.4 %collective-permute-done.21 = bf16[192,512]{1,0:T(8,128)(2,1)S(1)} collective-permute-done((bf16[192,512]{1,0:T(8,128)(2,1)S(1)}, bf16[192,512]{1,0:T(8,128)(2,1)S(1)}, u32[]{:S(2)}, u32[]{:S(2)}) %collective-permute-start.21) | collective-permute-done | bytes 196640 | tf_op jit(solution)/shard_map/ppermute | solution.py:427
  94.5 1.9 %collective-permute-done.20 = bf16[192,512]{1,0:T(8,128)(2,1)S(1)} collective-permute-done((bf16[192,512]{1,0:T(8,128)(2,1)S(1)}, bf16[192,512]{1,0:T(8,128)(2,1)S(1)}, u32[]{:S(2)}, u32[]{:S(2)}) %collective-permute-start.20) | collective-permute-done | bytes 196640 | tf_op jit(solution)/shard_map/ppermute | solution.py:427
  96.4 5.2 %collective-permute-done.19 = bf16[192,512]{1,0:T(8,128)(2,1)S(1)} collective-permute-done((bf16[192,512]{1,0:T(8,128)(2,1)S(1)}, bf16[192,512]{1,0:T(8,128)(2,1)S(1)}, u32[]{:S(2)}, u32[]{:S(2)}) %collective-permute-start.19) | collective-permute-done | bytes 196640 | tf_op jit(solution)/shard_map/ppermute | solution.py:427
  101.6 1.7 %fusion.2 = bf16[192,512]{1,0:T(8,128)(2,1)} fusion(bf16[192,512]{1,0:T(8,128)(2,1)S(1)} %collective-permute-done.21, bf16[192,512]{1,0:T(8,128)(2,1)S(1)} %collective-permute-done.20, bf16[192,512]{1,0:T(8,128)(2,1)S(1)} %collective-permute-done.19, bf16[4,192,512]{2,1,0:T(8,128)(2,1)S(1)} %collective-permute-done.18, bf16[4,192,512]{2,1,0:T(8,128)(2,1)} %get-tuple-element.95), kind=kLoop, calls=%fused_computation.3 | loop fusion | flops 983040 | bytes 1179648 | tf_op jit(solution)/shard_map/convert_element_type | solution.py:428
  103.3 0.0 all-to-all-done
  103.3 1.0 %reduce_sum.30 = bf16[256,512]{1,0:T(8,128)(2,1)} reduce(bf16[8,256,512]{2,1,0:T(8,128)(2,1)S(1)} %all-to-all-done, bf16[]{:T(256)} %constant.85.clone.1), dimensions={0}, to_apply=%region_0.1 | reduce | flops 917504 | bytes 2359298 | tf_op jit(solution)/shard_map/reduce_sum | solution.py:516
  (16 shorter events, 0.1 us)
Async XLA Ops:
  3.1 17.3 %collective-permute-start.5 = (bf16[1056,128]{1,0:T(8,128)(2,1)S(1)}, bf16[1056,128]{1,0:T(8,128)(2,1)S(1)}, u32[]{:S(2)}, u32[]{:S(2)}) collective-permute-start(bf16[1056,128]{1,0:T(8,128)(2,1)S(1)} %concatenate.10.refs_0_), channel_id=1, source_target_pairs={{0,8},{8,16},{16,24},{24,32},{32,40},{40,48},{48,56},{56,0},{64,72... | collective-permute-start | bytes 811016 | tf_op jit(solution)/shard_map/ppermute | solution.py:433
  4.8 15.6 %collective-permute-start.6 = (bf16[1056,128]{1,0:T(8,128)(2,1)S(1)}, bf16[1056,128]{1,0:T(8,128)(2,1)S(1)}, u32[]{:S(2)}, u32[]{:S(2)}) collective-permute-start(bf16[1056,128]{1,0:T(8,128)(2,1)S(1)} %concatenate.10.refs_0_), channel_id=1, source_target_pairs={{0,56},{8,0},{16,8},{24,16},{32,24},{40,32},{48,40},{56,48},{64,12... | collective-permute-start | bytes 811016 | tf_op jit(solution)/shard_map/ppermute | solution.py:433
  4.8 21.3 %collective-permute-start.7 = (bf16[1056,128]{1,0:T(8,128)(2,1)S(1)}, bf16[1056,128]{1,0:T(8,128)(2,1)S(1)}, u32[]{:S(2)}, u32[]{:S(2)}) collective-permute-start(bf16[1056,128]{1,0:T(8,128)(2,1)S(1)} %concatenate.10.refs_0_), channel_id=1, source_target_pairs={{0,16},{8,24},{16,32},{24,40},{32,48},{40,56},{48,0},{56,8},{64,80... | collective-permute-start | bytes 811016 | tf_op jit(solution)/shard_map/ppermute | solution.py:433
  9.0 17.1 %collective-permute-start.8 = (bf16[1056,128]{1,0:T(8,128)(2,1)S(1)}, bf16[1056,128]{1,0:T(8,128)(2,1)S(1)}, u32[]{:S(2)}, u32[]{:S(2)}) collective-permute-start(bf16[1056,128]{1,0:T(8,128)(2,1)S(1)} %concatenate.10.refs_0_), channel_id=1, source_target_pairs={{0,48},{8,56},{16,0},{24,8},{32,16},{40,24},{48,32},{56,40},{64,11... | collective-permute-start | bytes 811016 | tf_op jit(solution)/shard_map/ppermute | solution.py:433
  11.6 22.2 %copy-start.2 = (s32[32]{0:T(128)S(1)}, s32[32]{0:T(128)}, u32[]{:S(2)}) copy-start(s32[32]{0:T(128)} %param.40) | copy-start | bytes 388
  26.1 9.2 %collective-permute-start.9 = (bf16[1056,128]{1,0:T(8,128)(2,1)S(1)}, bf16[1056,128]{1,0:T(8,128)(2,1)}, u32[]{:S(2)}, u32[]{:S(2)}) collective-permute-start(bf16[1056,128]{1,0:T(8,128)(2,1)S(1)} %collective-permute-done.7.refs_3_), channel_id=1, source_target_pairs={{0,8},{8,16},{16,24},{24,32},{32,40},{40,48},{48,56},{56,0},{64,72... | collective-permute-start | bytes 811016 | tf_op jit(solution)/shard_map/ppermute | solution.py:433
  28.8 6.5 %collective-permute-start.10 = (bf16[1056,128]{1,0:T(8,128)(2,1)S(1)}, bf16[1056,128]{1,0:T(8,128)(2,1)}, u32[]{:S(2)}, u32[]{:S(2)}) collective-permute-start(bf16[1056,128]{1,0:T(8,128)(2,1)S(1)} %collective-permute-done.8.refs_4_), channel_id=1, source_target_pairs={{0,56},{8,0},{16,8},{24,16},{32,24},{40,32},{48,40},{56,48},{64,12... | collective-permute-start | bytes 811016 | tf_op jit(solution)/shard_map/ppermute | solution.py:433
  30.2 10.4 %collective-permute-start.11 = (bf16[1056,128]{1,0:T(8,128)(2,1)}, bf16[1056,128]{1,0:T(8,128)(2,1)}, u32[]{:S(2)}, u32[]{:S(2)}) collective-permute-start(bf16[1056,128]{1,0:T(8,128)(2,1)} %get-tuple-element.71), channel_id=1, source_target_pairs={{0,16},{8,56},{16,32},{24,8},{32,48},{40,24},{48,0},{56,40},{64,80... | collective-permute-start | bytes 811016 | tf_op jit(solution)/shard_map/ppermute | solution.py:441
  31.1 9.5 %collective-permute-start.12 = (bf16[1056,128]{1,0:T(8,128)(2,1)}, bf16[1056,128]{1,0:T(8,128)(2,1)S(1)}, u32[]{:S(2)}, u32[]{:S(2)}) collective-permute-start(bf16[1056,128]{1,0:T(8,128)(2,1)} %get-tuple-element.72), channel_id=1, source_target_pairs={{0,64},{8,72},{16,80},{24,88},{32,96},{40,104},{48,112},{56,120},{... | collective-permute-start | bytes 811016 | tf_op jit(solution)/shard_map/ppermute | solution.py:446
  32.3 8.3 %collective-permute-start.13 = (bf16[1056,128]{1,0:T(8,128)(2,1)}, bf16[1056,128]{1,0:T(8,128)(2,1)S(1)}, u32[]{:S(2)}, u32[]{:S(2)}) collective-permute-start(bf16[1056,128]{1,0:T(8,128)(2,1)} %get-tuple-element.73), channel_id=1, source_target_pairs={{0,192},{8,200},{16,208},{24,216},{32,224},{40,232},{48,240},{56,2... | collective-permute-start | bytes 811016 | tf_op jit(solution)/shard_map/ppermute | solution.py:446
  40.6 1.5 %copy-start = (bf16[1056,128]{1,0:T(8,128)(2,1)}, bf16[1056,128]{1,0:T(8,128)(2,1)S(1)}, u32[]{:S(2)}) copy-start(bf16[1056,128]{1,0:T(8,128)(2,1)S(1)} %collective-permute-done.12.refs_8_) | copy-start | bytes 811012
  40.6 1.5 %copy-start.1 = (bf16[1056,128]{1,0:T(8,128)(2,1)}, bf16[1056,128]{1,0:T(8,128)(2,1)S(1)}, u32[]{:S(2)}) copy-start(bf16[1056,128]{1,0:T(8,128)(2,1)S(1)} %collective-permute-done.13.refs_9_) | copy-start | bytes 811012
  42.8 23.2 %collective-permute-start.14 = (bf16[1056,128]{1,0:T(8,128)(2,1)}, bf16[1056,128]{1,0:T(8,128)(2,1)}, u32[]{:S(2)}, u32[]{:S(2)}) collective-permute-start(bf16[1056,128]{1,0:T(8,128)(2,1)} %get-tuple-element.86), channel_id=1, source_target_pairs={{0,64},{8,72},{16,80},{24,88},{32,96},{40,104},{48,112},{56,120},{... | collective-permute-start | bytes 811016 | tf_op jit(solution)/shard_map/ppermute | solution.py:446
  43.5 26.9 %collective-permute-start.15 = (bf16[1056,128]{1,0:T(8,128)(2,1)}, bf16[1056,128]{1,0:T(8,128)(2,1)}, u32[]{:S(2)}, u32[]{:S(2)}) collective-permute-start(bf16[1056,128]{1,0:T(8,128)(2,1)} %get-tuple-element.87), channel_id=1, source_target_pairs={{0,192},{8,200},{16,208},{24,216},{32,224},{40,232},{48,240},{56,2... | collective-permute-start | bytes 811016 | tf_op jit(solution)/shard_map/ppermute | solution.py:446
  54.1 16.4 %collective-permute-start.16 = (bf16[1056,128]{1,0:T(8,128)(2,1)}, bf16[1056,128]{1,0:T(8,128)(2,1)}, u32[]{:S(2)}, u32[]{:S(2)}) collective-permute-start(bf16[1056,128]{1,0:T(8,128)(2,1)} %get-tuple-element.88), channel_id=1, source_target_pairs={{0,128},{8,136},{16,144},{24,152},{32,160},{40,168},{48,176},{56,1... | collective-permute-start | bytes 811016 | tf_op jit(solution)/shard_map/ppermute | solution.py:446
  55.2 15.4 %collective-permute-start.17 = (bf16[1056,128]{1,0:T(8,128)(2,1)}, bf16[1056,128]{1,0:T(8,128)(2,1)}, u32[]{:S(2)}, u32[]{:S(2)}) collective-permute-start(bf16[1056,128]{1,0:T(8,128)(2,1)} %get-tuple-element.89), channel_id=1, source_target_pairs={{0,128},{8,136},{16,144},{24,152},{32,160},{40,168},{48,176},{56,1... | collective-permute-start | bytes 811016 | tf_op jit(solution)/shard_map/ppermute | solution.py:446
  57.1 46.3 %all-to-all-start = ((bf16[8,256,512]{2,1,0:T(8,128)(2,1)}), bf16[8,256,512]{2,1,0:T(8,128)(2,1)S(1)}, u32[]{:S(2)}, u32[]{:S(2)}) async-start(bf16[8,256,512]{2,1,0:T(8,128)(2,1)} %resident_rows.1), calls=%async_computation | async-start | bytes 4194304 | tf_op jit(solution)/shard_map/all_to_all | solution.py:498
  78.8 6.2 %collective-permute-start.18 = (bf16[4,192,512]{2,1,0:T(8,128)(2,1)}, bf16[4,192,512]{2,1,0:T(8,128)(2,1)S(1)}, u32[]{:S(2)}, u32[]{:S(2)}) collective-permute-start(bf16[4,192,512]{2,1,0:T(8,128)(2,1)} %get-tuple-element.96), channel_id=1, source_target_pairs={{0,1},{1,0},{2,3},{3,2},{4,5},{5,4},{6,7},{7,6},{8,9},{9,8},{10,11... | collective-permute-start | bytes 2359304 | tf_op jit(solution)/shard_map/ppermute | solution.py:416
  86.2 8.2 %collective-permute-start.21 = (bf16[192,512]{1,0:T(8,128)(2,1)S(1)}, bf16[192,512]{1,0:T(8,128)(2,1)S(1)}, u32[]{:S(2)}, u32[]{:S(2)}) collective-permute-start(bf16[192,512]{1,0:T(8,128)(2,1)S(1)} %get-tuple-element.101), channel_id=1, source_target_pairs={{0,6},{1,7},{2,0},{3,1},{4,2},{5,3},{6,4},{7,5},{8,14},{9,15},{10,... | collective-permute-start | bytes 589832 | tf_op jit(solution)/shard_map/ppermute | solution.py:427
  89.0 7.3 %collective-permute-start.20 = (bf16[192,512]{1,0:T(8,128)(2,1)S(1)}, bf16[192,512]{1,0:T(8,128)(2,1)S(1)}, u32[]{:S(2)}, u32[]{:S(2)}) collective-permute-start(bf16[192,512]{1,0:T(8,128)(2,1)S(1)} %get-tuple-element.102), channel_id=1, source_target_pairs={{0,4},{1,5},{2,6},{3,7},{4,0},{5,1},{6,2},{7,3},{8,12},{9,13},{10,... | collective-permute-start | bytes 589832 | tf_op jit(solution)/shard_map/ppermute | solution.py:427
  89.4 12.2 %collective-permute-start.19 = (bf16[192,512]{1,0:T(8,128)(2,1)S(1)}, bf16[192,512]{1,0:T(8,128)(2,1)S(1)}, u32[]{:S(2)}, u32[]{:S(2)}) collective-permute-start(bf16[192,512]{1,0:T(8,128)(2,1)S(1)} %get-tuple-element.100), channel_id=1, source_target_pairs={{0,2},{1,3},{2,4},{3,5},{4,6},{5,7},{6,0},{7,1},{8,10},{9,11},{10,... | collective-permute-start | bytes 589832 | tf_op jit(solution)/shard_map/ppermute | solution.py:427
where the time goes:
time: 106 us; the launch traced here: 104 us
  starting transfers between devices  43.5 us (41%)
  waiting for transfers between devices  29.1 us (27%)
  Pallas kernels  20.3 us (19%)
  other arithmetic  6.14 us (6%)
  local copies, waits for them, and re-layouts  3.06 us (3%)
  between operations  2.07 us (2%)
    ppermute x6, starting transfers between devices, along_x(): lax.ppermute(array, 'rep', [(x * NZ + z, (x + shift) % NX * NZ + z) for x...  16.9 us
    ppermute x3, waiting for transfers between devices, reduce_out(): lax.ppermute(chip[k].astype(BF16), 'tp', shifted).astype(F32)  11.5 us
    ppermute x6, starting transfers between devices, along_z(): return lax.ppermute(array, 'rep', pairs)  9.4 us
    pallas_call x1, Pallas kernels, resident_rows(): pl.pallas_call(resident_kernel, grid=(slots,), in_specs=[pl.BlockSpec(mem...  8.72 us
    all_to_all x1, starting transfers between devices, on_device(): res_parts = lax.all_to_all(res_parts, 'tp', 0, 0, tiled=True)  8.35 us
    pallas_call x1, Pallas kernels, slot_rows(): pl.pallas_call(slot_kernel, grid=(slots,), in_specs=[pl.BlockSpec(memory_...  8.24 us
    ppermute x6, waiting for transfers between devices, along_z(): return lax.ppermute(array, 'rep', pairs)  5.68 us
    ppermute x1, waiting for transfers between devices, across_z(): return lax.ppermute(array, 'rep', pairs)  5.27 us
  transfers between devices with their start and end apart: 18, of which 8 were waited for; matrix products, arithmetic and copies ran while one was open for 5% of the time, Pallas kernels for 18%

commit v1 on v0

--- a/solution.py
+++ b/solution.py
@@ -279,7 +279,7 @@
         functools.partial(forward_kernel, sends, offsets),
         in_specs=[pl.BlockSpec(memory_space=pltpu.SMEM)]
         + [pl.BlockSpec(memory_space=pl.ANY)] * len(packets),
-        out_specs=[pl.BlockSpec(memory_space=pl.ANY)] * count,
+        out_specs=[pl.BlockSpec(memory_space=pltpu.VMEM)] * count,
         out_shape=[jax.ShapeDtypeStruct((PACK, 128), BF16)] * count,
         scratch_shapes=[pltpu.SemaphoreType.DMA((count,))],
         cost_estimate=pl.CostEstimate(flops=0, bytes_accessed=3_000_000, transcendentals=0),

time: 106 us -> 97.9 us (0.924)
  the two profiles are of different devices: /device:TPU:33 before, /device:TPU:1 now
where the time goes in v1:
time: 97.9 us; the launch traced here: 97.6 us
  starting transfers between devices  41.7 us (43%)
  waiting for transfers between devices  23.3 us (24%)
  Pallas kernels  21 us (21%)
  other arithmetic  6.14 us (6%)
  local copies, waits for them, and re-layouts  3.06 us (3%)
  between operations  2.08 us (2%)
    ppermute x6, starting transfers between devices, along_z(): return lax.ppermute(array, 'rep', pairs)  12.8 us
    ppermute x3, waiting for transfers between devices, reduce_out(): lax.ppermute(chip[k].astype(BF16), 'tp', shifted).astype(F32)  11.5 us
    all_to_all x1, starting transfers between devices, on_device(): res_parts = lax.all_to_all(res_parts, 'tp', 0, 0, tiled=True)  8.77 us
    pallas_call x1, Pallas kernels, resident_rows(): pl.pallas_call(resident_kernel, grid=(slots,), in_specs=[pl.BlockSpec(mem...  8.72 us
    ppermute x6, starting transfers between devices, along_x(): lax.ppermute(array, 'rep', [(x * NZ + z, (x + shift) % NX * NZ + z) for x...  8.4 us
    pallas_call x1, Pallas kernels, slot_rows(): pl.pallas_call(slot_kernel, grid=(slots,), in_specs=[pl.BlockSpec(memory_...  8.24 us
    ppermute x1, starting transfers between devices, across_cores(): return lax.ppermute(array, 'tp', [(t, t ^ 1) for t in range(2 * NY)])  4.4 us
    ppermute x3, starting transfers between devices, reduce_out(): lax.ppermute(chip[k].astype(BF16), 'tp', shifted).astype(F32)  3.85 us
  transfers between devices with their start and end apart: 18, of which 7 were waited for; matrix products, arithmetic and copies ran while one was open for 6% of the time, Pallas kernels for 19%

profile of v1, /device:TPU:1, one launch (start us, length us, event | category | flops | bytes accessed | tf_op | source)
XLA Modules:
  0.0 97.6 jit_solution(18035727484619314708)
XLA Ops:
  0.6 0.7 reshape.104
  1.3 0.7 reshape.105
  2.0 1.0 %concatenate.10.refs_0_ = bf16[1056,128]{1,0:T(8,128)(2,1)S(1)} concatenate(bf16[1024,128]{1,0:T(8,128)(2,1)} %bitcast.26, bf16[24,128]{1,0:T(8,128)(2,1)S(1)} %reshape.104, bf16[6,128]{1,0:T(8,128)(2,1)S(1)} %reshape.105, bf16[2,128]{1,0:T(2,128)(2,1)S(1)} %broadcast_in_dim.30), dimensions={0} | concatenate | bytes 540672 | tf_op jit(solution)/shard_map/concatenate | solution.py:462
  3.1 2.5 %collective-permute-start.5 = (bf16[1056,128]{1,0:T(8,128)(2,1)S(1)}, bf16[1056,128]{1,0:T(8,128)(2,1)S(1)}, u32[]{:S(2)}, u32[]{:S(2)}) collective-permute-start(bf16[1056,128]{1,0:T(8,128)(2,1)S(1)} %concatenate.10.refs_0_), channel_id=1, source_target_pairs={{0,8},{8,16},{16,24},{24,32},{32,40},{40,48},{48,56},{56,0},{64,72... | collective-permute-start | bytes 811016 | tf_op jit(solution)/shard_map/ppermute | solution.py:433
  5.6 4.0 %collective-permute-start.6 = (bf16[1056,128]{1,0:T(8,128)(2,1)S(1)}, bf16[1056,128]{1,0:T(8,128)(2,1)S(1)}, u32[]{:S(2)}, u32[]{:S(2)}) collective-permute-start(bf16[1056,128]{1,0:T(8,128)(2,1)S(1)} %concatenate.10.refs_0_), channel_id=1, source_target_pairs={{0,56},{8,0},{16,8},{24,16},{32,24},{40,32},{48,40},{56,48},{64,12... | collective-permute-start | bytes 811016 | tf_op jit(solution)/shard_map/ppermute | solution.py:433
  9.6 0.0 collective-permute-start.7
  9.6 3.6 %collective-permute-start.8 = (bf16[1056,128]{1,0:T(8,128)(2,1)S(1)}, bf16[1056,128]{1,0:T(8,128)(2,1)S(1)}, u32[]{:S(2)}, u32[]{:S(2)}) collective-permute-start(bf16[1056,128]{1,0:T(8,128)(2,1)S(1)} %concatenate.10.refs_0_), channel_id=1, source_target_pairs={{0,48},{8,56},{16,0},{24,8},{32,16},{40,24},{48,32},{56,40},{64,11... | collective-permute-start | bytes 811016 | tf_op jit(solution)/shard_map/ppermute | solution.py:433
  13.9 0.7 pad_add_fusion.info
  14.6 0.5 iota.40.blocks
  15.1 8.7 %resident_rows.1 = bf16[8,256,512]{2,1,0:T(8,128)(2,1)} custom-call(s32[1]{0:T(128)S(6)} %copy.36.count, s32[8]{0:T(128)} %iota.40.blocks, bf16[1024,4096]{1,0:T(8,128)(2,1)} %out_w.3, bf16[4,16,64,128]{3,2,1,0:T(8,128)(2,1)} %state.1, bf16[3,4,1024]{2,1,0:T(4,128)(2,1)} %bitcast.28, bf16[4,3,2,128]{3,2,1,0:T(2,128)(2,1)} %conv_bc.1, ...), custom_call_target="tpu_custom_call" | custom-call | flops 3000000000 | bytes 16000000 | tf_op jit(solution)/shard_map/resident_rows/pallas_call | solution.py:211
  23.9 0.0 collective-permute-done.5.refs_1_
  23.9 2.5 %collective-permute-done.8.refs_4_ = bf16[1056,128]{1,0:T(8,128)(2,1)S(1)} collective-permute-done((bf16[1056,128]{1,0:T(8,128)(2,1)S(1)}, bf16[1056,128]{1,0:T(8,128)(2,1)S(1)}, u32[]{:S(2)}, u32[]{:S(2)}) %collective-permute-start.8) | collective-permute-done | bytes 270368 | tf_op jit(solution)/shard_map/ppermute | solution.py:433
  26.4 2.2 %collective-permute-start.9 = (bf16[1056,128]{1,0:T(8,128)(2,1)S(1)}, bf16[1056,128]{1,0:T(8,128)(2,1)}, u32[]{:S(2)}, u32[]{:S(2)}) collective-permute-start(bf16[1056,128]{1,0:T(8,128)(2,1)S(1)} %collective-permute-done.7.refs_3_), channel_id=1, source_target_pairs={{0,8},{8,16},{16,24},{24,32},{32,40},{40,48},{48,56},{56,0},{64,72... | collective-permute-start | bytes 811016 | tf_op jit(solution)/shard_map/ppermute | solution.py:433
  28.5 0.5 collective-permute-start.10
  29.1 1.6 %forward.4 = (bf16[1056,128]{1,0:T(8,128)(2,1)}, bf16[1056,128]{1,0:T(8,128)(2,1)}, bf16[1056,128]{1,0:T(8,128)(2,1)}) custom-call(s32[33]{0:T(128)S(1)} %pad_add_fusion.info, bf16[1056,128]{1,0:T(8,128)(2,1)S(1)} %concatenate.10.refs_0_, bf16[1056,128]{1,0:T(8,128)(2,1)S(1)} %collective-permute-done.5.refs_1_, ...), custom_call_target="tpu_custom_call" | custom-call | bytes 3000000 | tf_op jit(solution)/shard_map/forward/pallas_call | solution.py:278
  30.7 3.5 %collective-permute-start.11 = (bf16[1056,128]{1,0:T(8,128)(2,1)}, bf16[1056,128]{1,0:T(8,128)(2,1)}, u32[]{:S(2)}, u32[]{:S(2)}) collective-permute-start(bf16[1056,128]{1,0:T(8,128)(2,1)} %get-tuple-element.71), channel_id=1, source_target_pairs={{0,16},{8,56},{16,32},{24,8},{32,48},{40,24},{48,0},{56,40},{64,80... | collective-permute-start | bytes 811016 | tf_op jit(solution)/shard_map/ppermute | solution.py:441
  34.2 1.2 %collective-permute-start.12 = (bf16[1056,128]{1,0:T(8,128)(2,1)}, bf16[1056,128]{1,0:T(8,128)(2,1)S(1)}, u32[]{:S(2)}, u32[]{:S(2)}) collective-permute-start(bf16[1056,128]{1,0:T(8,128)(2,1)} %get-tuple-element.72), channel_id=1, source_target_pairs={{0,64},{8,72},{16,80},{24,88},{32,96},{40,104},{48,112},{56,120},{... | collective-permute-start | bytes 811016 | tf_op jit(solution)/shard_map/ppermute | solution.py:446
  35.4 1.5 %collective-permute-start.13 = (bf16[1056,128]{1,0:T(8,128)(2,1)}, bf16[1056,128]{1,0:T(8,128)(2,1)S(1)}, u32[]{:S(2)}, u32[]{:S(2)}) collective-permute-start(bf16[1056,128]{1,0:T(8,128)(2,1)} %get-tuple-element.73), channel_id=1, source_target_pairs={{0,192},{8,200},{16,208},{24,216},{32,224},{40,232},{48,240},{56,2... | collective-permute-start | bytes 811016 | tf_op jit(solution)/shard_map/ppermute | solution.py:446
  36.9 0.1 eq.37
  37.0 0.1 convert_reduce_fusion
  37.1 0.6 fusion.12
  38.4 0.0 collective-permute-done.10.refs_6_
  38.4 3.4 %collective-permute-done.11.refs_7_ = bf16[1056,128]{1,0:T(8,128)(2,1)} collective-permute-done((bf16[1056,128]{1,0:T(8,128)(2,1)}, bf16[1056,128]{1,0:T(8,128)(2,1)}, u32[]{:S(2)}, u32[]{:S(2)}) %collective-permute-start.11) | collective-permute-done | bytes 270368 | tf_op jit(solution)/shard_map/ppermute | solution.py:441
  41.8 0.0 collective-permute-done.12.refs_8_
  41.8 0.0 collective-permute-done.13.refs_9_
  41.9 1.9 %forward.5 = (bf16[1056,128]{1,0:T(8,128)(2,1)}, bf16[1056,128]{1,0:T(8,128)(2,1)}, bf16[1056,128]{1,0:T(8,128)(2,1)}, bf16[1056,128]{1,0:T(8,128)(2,1)}) custom-call(s32[33]{0:T(128)S(1)} %pad_add_fusion.info, bf16[1056,128]{1,0:T(8,128)(2,1)S(1)} %concatenate.10.refs_0_, bf16[1056,128]{1,0:T(8,128)(2,1)S(1)} %collective-permute-done.5.refs_1_, ...), custom_call_target="tpu_custom_call" | custom-call | bytes 3000000 | tf_op jit(solution)/shard_map/forward/pallas_call | solution.py:278
  43.8 0.8 conditional.1
  43.8 0.5 blank.1
  44.6 1.3 %collective-permute-start.14 = (bf16[1056,128]{1,0:T(8,128)(2,1)}, bf16[1056,128]{1,0:T(8,128)(2,1)}, u32[]{:S(2)}, u32[]{:S(2)}) collective-permute-start(bf16[1056,128]{1,0:T(8,128)(2,1)} %get-tuple-element.86), channel_id=1, source_target_pairs={{0,64},{8,72},{16,80},{24,88},{32,96},{40,104},{48,112},{56,120},{... | collective-permute-start | bytes 811016 | tf_op jit(solution)/shard_map/ppermute | solution.py:446
  45.9 1.5 %collective-permute-start.15 = (bf16[1056,128]{1,0:T(8,128)(2,1)}, bf16[1056,128]{1,0:T(8,128)(2,1)}, u32[]{:S(2)}, u32[]{:S(2)}) collective-permute-start(bf16[1056,128]{1,0:T(8,128)(2,1)} %get-tuple-element.87), channel_id=1, source_target_pairs={{0,192},{8,200},{16,208},{24,216},{32,224},{40,232},{48,240},{56,2... | collective-permute-start | bytes 811016 | tf_op jit(solution)/shard_map/ppermute | solution.py:446
  47.3 1.5 %collective-permute-start.16 = (bf16[1056,128]{1,0:T(8,128)(2,1)}, bf16[1056,128]{1,0:T(8,128)(2,1)}, u32[]{:S(2)}, u32[]{:S(2)}) collective-permute-start(bf16[1056,128]{1,0:T(8,128)(2,1)} %get-tuple-element.88), channel_id=1, source_target_pairs={{0,128},{8,136},{16,144},{24,152},{32,160},{40,168},{48,176},{56,1... | collective-permute-start | bytes 811016 | tf_op jit(solution)/shard_map/ppermute | solution.py:446
  48.9 1.4 %collective-permute-start.17 = (bf16[1056,128]{1,0:T(8,128)(2,1)}, bf16[1056,128]{1,0:T(8,128)(2,1)}, u32[]{:S(2)}, u32[]{:S(2)}) collective-permute-start(bf16[1056,128]{1,0:T(8,128)(2,1)} %get-tuple-element.89), channel_id=1, source_target_pairs={{0,128},{8,136},{16,144},{24,152},{32,160},{40,168},{48,176},{56,1... | collective-permute-start | bytes 811016 | tf_op jit(solution)/shard_map/ppermute | solution.py:446
  50.3 8.8 %all-to-all-start = ((bf16[8,256,512]{2,1,0:T(8,128)(2,1)}), bf16[8,256,512]{2,1,0:T(8,128)(2,1)S(1)}, u32[]{:S(2)}, u32[]{:S(2)}) async-start(bf16[8,256,512]{2,1,0:T(8,128)(2,1)} %resident_rows.1), calls=%async_computation | async-start | bytes 4194304 | tf_op jit(solution)/shard_map/all_to_all | solution.py:498
  59.1 0.6 pad_add_fusion.1.blocks
  59.7 0.0 collective-permute-done.14.refs_10_
  59.7 3.7 %collective-permute-done.17.refs_13_ = bf16[1056,128]{1,0:T(8,128)(2,1)} collective-permute-done((bf16[1056,128]{1,0:T(8,128)(2,1)}, bf16[1056,128]{1,0:T(8,128)(2,1)}, u32[]{:S(2)}, u32[]{:S(2)}) %collective-permute-start.17) | collective-permute-done | bytes 270368 | tf_op jit(solution)/shard_map/ppermute | solution.py:446
  63.4 8.2 %slot_rows.1 = (bf16[4,192,512]{2,1,0:T(8,128)(2,1)}, bf16[4,192,512]{2,1,0:T(8,128)(2,1)}, bf16[3,16,64,128]{3,2,1,0:T(8,128)(2,1)}) custom-call(s32[33]{0:T(128)S(1)} %pad_add_fusion.info, s32[8]{0:T(128)} %pad_add_fusion.1.blocks, bf16[1024,4096]{1,0:T(8,128)(2,1)} %out_w.3, bf16[1056,128]{1,0:T(8,128)(2,1)S(1)} %concatenate.10.refs_0_, ...), custom_call_target="tpu_custom_call" | custom-call | flops 3000000000 | bytes 20000000 | tf_op jit(solution)/shard_map/slot_rows/pallas_call | solution.py:392
  71.7 4.4 %collective-permute-start.18 = (bf16[4,192,512]{2,1,0:T(8,128)(2,1)}, bf16[4,192,512]{2,1,0:T(8,128)(2,1)S(1)}, u32[]{:S(2)}, u32[]{:S(2)}) collective-permute-start(bf16[4,192,512]{2,1,0:T(8,128)(2,1)} %get-tuple-element.96), channel_id=1, source_target_pairs={{0,1},{1,0},{2,3},{3,2},{4,5},{5,4},{6,7},{7,6},{8,9},{9,8},{10,11... | collective-permute-start | bytes 2359304 | tf_op jit(solution)/shard_map/ppermute | solution.py:416
  76.0 2.1 %collective-permute-done.18 = bf16[4,192,512]{2,1,0:T(8,128)(2,1)S(1)} collective-permute-done((bf16[4,192,512]{2,1,0:T(8,128)(2,1)}, bf16[4,192,512]{2,1,0:T(8,128)(2,1)S(1)}, u32[]{:S(2)}, u32[]{:S(2)}) %collective-permute-start.18) | collective-permute-done | bytes 786464 | tf_op jit(solution)/shard_map/ppermute | solution.py:416
  78.2 1.3 %fusion.3 = (bf16[192,512]{1,0:T(8,128)(2,1)S(1)}, bf16[192,512]{1,0:T(8,128)(2,1)S(1)}, bf16[192,512]{1,0:T(8,128)(2,1)S(1)}) fusion(bf16[4,192,512]{2,1,0:T(8,128)(2,1)S(1)} %collective-permute-done.18, bf16[4,192,512]{2,1,0:T(8,128)(2,1)} %get-tuple-element.95), kind=kLoop, calls=%fused_computation.7 | loop fusion | flops 1179648 | bytes 1769472 | tf_op jit(solution)/shard_map/convert_element_type | solution.py:427
  79.4 2.8 %collective-permute-start.21 = (bf16[192,512]{1,0:T(8,128)(2,1)S(1)}, bf16[192,512]{1,0:T(8,128)(2,1)S(1)}, u32[]{:S(2)}, u32[]{:S(2)}) collective-permute-start(bf16[192,512]{1,0:T(8,128)(2,1)S(1)} %get-tuple-element.101), channel_id=1, source_target_pairs={{0,6},{1,7},{2,0},{3,1},{4,2},{5,3},{6,4},{7,5},{8,14},{9,15},{10,... | collective-permute-start | bytes 589832 | tf_op jit(solution)/shard_map/ppermute | solution.py:427
  82.3 0.3 collective-permute-start.20
  82.6 0.7 collective-permute-start.19
  83.3 4.8 %collective-permute-done.21 = bf16[192,512]{1,0:T(8,128)(2,1)S(1)} collective-permute-done((bf16[192,512]{1,0:T(8,128)(2,1)S(1)}, bf16[192,512]{1,0:T(8,128)(2,1)S(1)}, u32[]{:S(2)}, u32[]{:S(2)}) %collective-permute-start.21) | collective-permute-done | bytes 196640 | tf_op jit(solution)/shard_map/ppermute | solution.py:427
  88.1 1.5 %collective-permute-done.20 = bf16[192,512]{1,0:T(8,128)(2,1)S(1)} collective-permute-done((bf16[192,512]{1,0:T(8,128)(2,1)S(1)}, bf16[192,512]{1,0:T(8,128)(2,1)S(1)}, u32[]{:S(2)}, u32[]{:S(2)}) %collective-permute-start.20) | collective-permute-done | bytes 196640 | tf_op jit(solution)/shard_map/ppermute | solution.py:427
  89.6 5.2 %collective-permute-done.19 = bf16[192,512]{1,0:T(8,128)(2,1)S(1)} collective-permute-done((bf16[192,512]{1,0:T(8,128)(2,1)S(1)}, bf16[192,512]{1,0:T(8,128)(2,1)S(1)}, u32[]{:S(2)}, u32[]{:S(2)}) %collective-permute-start.19) | collective-permute-done | bytes 196640 | tf_op jit(solution)/shard_map/ppermute | solution.py:427
  94.8 1.7 %fusion.2 = bf16[192,512]{1,0:T(8,128)(2,1)} fusion(bf16[192,512]{1,0:T(8,128)(2,1)S(1)} %collective-permute-done.21, bf16[192,512]{1,0:T(8,128)(2,1)S(1)} %collective-permute-done.20, bf16[192,512]{1,0:T(8,128)(2,1)S(1)} %collective-permute-done.19, bf16[4,192,512]{2,1,0:T(8,128)(2,1)S(1)} %collective-permute-done.18, bf16[4,192,512]{2,1,0:T(8,128)(2,1)} %get-tuple-element.95), kind=kLoop, calls=%fused_computation.3 | loop fusion | flops 983040 | bytes 1179648 | tf_op jit(solution)/shard_map/convert_element_type | solution.py:428
  96.5 1.0 %reduce_sum.30 = bf16[256,512]{1,0:T(8,128)(2,1)} reduce(bf16[8,256,512]{2,1,0:T(8,128)(2,1)S(1)} %all-to-all-done, bf16[]{:T(256)} %constant.85.clone.1), dimensions={0}, to_apply=%region_0.1 | reduce | flops 917504 | bytes 2359298 | tf_op jit(solution)/shard_map/reduce_sum | solution.py:516
  (16 shorter events, 0.1 us)
Async XLA Ops:
  3.1 20.8 %collective-permute-start.5 = (bf16[1056,128]{1,0:T(8,128)(2,1)S(1)}, bf16[1056,128]{1,0:T(8,128)(2,1)S(1)}, u32[]{:S(2)}, u32[]{:S(2)}) collective-permute-start(bf16[1056,128]{1,0:T(8,128)(2,1)S(1)} %concatenate.10.refs_0_), channel_id=1, source_target_pairs={{0,8},{8,16},{16,24},{24,32},{32,40},{40,48},{48,56},{56,0},{64,72... | collective-permute-start | bytes 811016 | tf_op jit(solution)/shard_map/ppermute | solution.py:433
  5.6 18.3 %collective-permute-start.6 = (bf16[1056,128]{1,0:T(8,128)(2,1)S(1)}, bf16[1056,128]{1,0:T(8,128)(2,1)S(1)}, u32[]{:S(2)}, u32[]{:S(2)}) collective-permute-start(bf16[1056,128]{1,0:T(8,128)(2,1)S(1)} %concatenate.10.refs_0_), channel_id=1, source_target_pairs={{0,56},{8,0},{16,8},{24,16},{32,24},{40,32},{48,40},{56,48},{64,12... | collective-permute-start | bytes 811016 | tf_op jit(solution)/shard_map/ppermute | solution.py:433
  9.6 14.2 %collective-permute-start.7 = (bf16[1056,128]{1,0:T(8,128)(2,1)S(1)}, bf16[1056,128]{1,0:T(8,128)(2,1)S(1)}, u32[]{:S(2)}, u32[]{:S(2)}) collective-permute-start(bf16[1056,128]{1,0:T(8,128)(2,1)S(1)} %concatenate.10.refs_0_), channel_id=1, source_target_pairs={{0,16},{8,24},{16,32},{24,40},{32,48},{40,56},{48,0},{56,8},{64,80... | collective-permute-start | bytes 811016 | tf_op jit(solution)/shard_map/ppermute | solution.py:433
  9.6 16.7 %collective-permute-start.8 = (bf16[1056,128]{1,0:T(8,128)(2,1)S(1)}, bf16[1056,128]{1,0:T(8,128)(2,1)S(1)}, u32[]{:S(2)}, u32[]{:S(2)}) collective-permute-start(bf16[1056,128]{1,0:T(8,128)(2,1)S(1)} %concatenate.10.refs_0_), channel_id=1, source_target_pairs={{0,48},{8,56},{16,0},{24,8},{32,16},{40,24},{48,32},{56,40},{64,11... | collective-permute-start | bytes 811016 | tf_op jit(solution)/shard_map/ppermute | solution.py:433
  15.1 21.8 %copy-start.2 = (s32[32]{0:T(128)S(1)}, s32[32]{0:T(128)}, u32[]{:S(2)}) copy-start(s32[32]{0:T(128)} %param.40) | copy-start | bytes 388
  26.4 12.0 %collective-permute-start.9 = (bf16[1056,128]{1,0:T(8,128)(2,1)S(1)}, bf16[1056,128]{1,0:T(8,128)(2,1)}, u32[]{:S(2)}, u32[]{:S(2)}) collective-permute-start(bf16[1056,128]{1,0:T(8,128)(2,1)S(1)} %collective-permute-done.7.refs_3_), channel_id=1, source_target_pairs={{0,8},{8,16},{16,24},{24,32},{32,40},{40,48},{48,56},{56,0},{64,72... | collective-permute-start | bytes 811016 | tf_op jit(solution)/shard_map/ppermute | solution.py:433
  28.5 9.8 %collective-permute-start.10 = (bf16[1056,128]{1,0:T(8,128)(2,1)S(1)}, bf16[1056,128]{1,0:T(8,128)(2,1)}, u32[]{:S(2)}, u32[]{:S(2)}) collective-permute-start(bf16[1056,128]{1,0:T(8,128)(2,1)S(1)} %collective-permute-done.8.refs_4_), channel_id=1, source_target_pairs={{0,56},{8,0},{16,8},{24,16},{32,24},{40,32},{48,40},{56,48},{64,12... | collective-permute-start | bytes 811016 | tf_op jit(solution)/shard_map/ppermute | solution.py:433
  30.7 11.2 %collective-permute-start.11 = (bf16[1056,128]{1,0:T(8,128)(2,1)}, bf16[1056,128]{1,0:T(8,128)(2,1)}, u32[]{:S(2)}, u32[]{:S(2)}) collective-permute-start(bf16[1056,128]{1,0:T(8,128)(2,1)} %get-tuple-element.71), channel_id=1, source_target_pairs={{0,16},{8,56},{16,32},{24,8},{32,48},{40,24},{48,0},{56,40},{64,80... | collective-permute-start | bytes 811016 | tf_op jit(solution)/shard_map/ppermute | solution.py:441
  34.2 7.6 %collective-permute-start.12 = (bf16[1056,128]{1,0:T(8,128)(2,1)}, bf16[1056,128]{1,0:T(8,128)(2,1)S(1)}, u32[]{:S(2)}, u32[]{:S(2)}) collective-permute-start(bf16[1056,128]{1,0:T(8,128)(2,1)} %get-tuple-element.72), channel_id=1, source_target_pairs={{0,64},{8,72},{16,80},{24,88},{32,96},{40,104},{48,112},{56,120},{... | collective-permute-start | bytes 811016 | tf_op jit(solution)/shard_map/ppermute | solution.py:446
  35.4 6.5 %collective-permute-start.13 = (bf16[1056,128]{1,0:T(8,128)(2,1)}, bf16[1056,128]{1,0:T(8,128)(2,1)S(1)}, u32[]{:S(2)}, u32[]{:S(2)}) collective-permute-start(bf16[1056,128]{1,0:T(8,128)(2,1)} %get-tuple-element.73), channel_id=1, source_target_pairs={{0,192},{8,200},{16,208},{24,216},{32,224},{40,232},{48,240},{56,2... | collective-permute-start | bytes 811016 | tf_op jit(solution)/shard_map/ppermute | solution.py:446
  41.8 1.9 %copy-start = (bf16[1056,128]{1,0:T(8,128)(2,1)}, bf16[1056,128]{1,0:T(8,128)(2,1)S(1)}, u32[]{:S(2)}) copy-start(bf16[1056,128]{1,0:T(8,128)(2,1)S(1)} %collective-permute-done.12.refs_8_) | copy-start | bytes 811012
  41.8 1.9 %copy-start.1 = (bf16[1056,128]{1,0:T(8,128)(2,1)}, bf16[1056,128]{1,0:T(8,128)(2,1)S(1)}, u32[]{:S(2)}) copy-start(bf16[1056,128]{1,0:T(8,128)(2,1)S(1)} %collective-permute-done.13.refs_9_) | copy-start | bytes 811012
  44.6 15.1 %collective-permute-start.14 = (bf16[1056,128]{1,0:T(8,128)(2,1)}, bf16[1056,128]{1,0:T(8,128)(2,1)}, u32[]{:S(2)}, u32[]{:S(2)}) collective-permute-start(bf16[1056,128]{1,0:T(8,128)(2,1)} %get-tuple-element.86), channel_id=1, source_target_pairs={{0,64},{8,72},{16,80},{24,88},{32,96},{40,104},{48,112},{56,120},{... | collective-permute-start | bytes 811016 | tf_op jit(solution)/shard_map/ppermute | solution.py:446
  45.9 13.8 %collective-permute-start.15 = (bf16[1056,128]{1,0:T(8,128)(2,1)}, bf16[1056,128]{1,0:T(8,128)(2,1)}, u32[]{:S(2)}, u32[]{:S(2)}) collective-permute-start(bf16[1056,128]{1,0:T(8,128)(2,1)} %get-tuple-element.87), channel_id=1, source_target_pairs={{0,192},{8,200},{16,208},{24,216},{32,224},{40,232},{48,240},{56,2... | collective-permute-start | bytes 811016 | tf_op jit(solution)/shard_map/ppermute | solution.py:446
  47.3 12.3 %collective-permute-start.16 = (bf16[1056,128]{1,0:T(8,128)(2,1)}, bf16[1056,128]{1,0:T(8,128)(2,1)}, u32[]{:S(2)}, u32[]{:S(2)}) collective-permute-start(bf16[1056,128]{1,0:T(8,128)(2,1)} %get-tuple-element.88), channel_id=1, source_target_pairs={{0,128},{8,136},{16,144},{24,152},{32,160},{40,168},{48,176},{56,1... | collective-permute-start | bytes 811016 | tf_op jit(solution)/shard_map/ppermute | solution.py:446
  48.9 14.5 %collective-permute-start.17 = (bf16[1056,128]{1,0:T(8,128)(2,1)}, bf16[1056,128]{1,0:T(8,128)(2,1)}, u32[]{:S(2)}, u32[]{:S(2)}) collective-permute-start(bf16[1056,128]{1,0:T(8,128)(2,1)} %get-tuple-element.89), channel_id=1, source_target_pairs={{0,128},{8,136},{16,144},{24,152},{32,160},{40,168},{48,176},{56,1... | collective-permute-start | bytes 811016 | tf_op jit(solution)/shard_map/ppermute | solution.py:446
  50.3 46.2 %all-to-all-start = ((bf16[8,256,512]{2,1,0:T(8,128)(2,1)}), bf16[8,256,512]{2,1,0:T(8,128)(2,1)S(1)}, u32[]{:S(2)}, u32[]{:S(2)}) async-start(bf16[8,256,512]{2,1,0:T(8,128)(2,1)} %resident_rows.1), calls=%async_computation | async-start | bytes 4194304 | tf_op jit(solution)/shard_map/all_to_all | solution.py:498
  71.7 6.5 %collective-permute-start.18 = (bf16[4,192,512]{2,1,0:T(8,128)(2,1)}, bf16[4,192,512]{2,1,0:T(8,128)(2,1)S(1)}, u32[]{:S(2)}, u32[]{:S(2)}) collective-permute-start(bf16[4,192,512]{2,1,0:T(8,128)(2,1)} %get-tuple-element.96), channel_id=1, source_target_pairs={{0,1},{1,0},{2,3},{3,2},{4,5},{5,4},{6,7},{7,6},{8,9},{9,8},{10,11... | collective-permute-start | bytes 2359304 | tf_op jit(solution)/shard_map/ppermute | solution.py:416
  79.4 8.7 %collective-permute-start.21 = (bf16[192,512]{1,0:T(8,128)(2,1)S(1)}, bf16[192,512]{1,0:T(8,128)(2,1)S(1)}, u32[]{:S(2)}, u32[]{:S(2)}) collective-permute-start(bf16[192,512]{1,0:T(8,128)(2,1)S(1)} %get-tuple-element.101), channel_id=1, source_target_pairs={{0,6},{1,7},{2,0},{3,1},{4,2},{5,3},{6,4},{7,5},{8,14},{9,15},{10,... | collective-permute-start | bytes 589832 | tf_op jit(solution)/shard_map/ppermute | solution.py:427
  82.3 7.3 %collective-permute-start.20 = (bf16[192,512]{1,0:T(8,128)(2,1)S(1)}, bf16[192,512]{1,0:T(8,128)(2,1)S(1)}, u32[]{:S(2)}, u32[]{:S(2)}) collective-permute-start(bf16[192,512]{1,0:T(8,128)(2,1)S(1)} %get-tuple-element.102), channel_id=1, source_target_pairs={{0,4},{1,5},{2,6},{3,7},{4,0},{5,1},{6,2},{7,3},{8,12},{9,13},{10,... | collective-permute-start | bytes 589832 | tf_op jit(solution)/shard_map/ppermute | solution.py:427
  82.6 12.2 %collective-permute-start.19 = (bf16[192,512]{1,0:T(8,128)(2,1)S(1)}, bf16[192,512]{1,0:T(8,128)(2,1)S(1)}, u32[]{:S(2)}, u32[]{:S(2)}) collective-permute-start(bf16[192,512]{1,0:T(8,128)(2,1)S(1)} %get-tuple-element.100), channel_id=1, source_target_pairs={{0,2},{1,3},{2,4},{3,5},{4,6},{5,7},{6,0},{7,1},{8,10},{9,11},{10,... | collective-permute-start | bytes 589832 | tf_op jit(solution)/shard_map/ppermute | solution.py:427
